TPU v7x, 32 devices: a whole 2x2x4 slice. The times are simulated.
32 devices in a mesh: section: 4 (over z), dp: 8 (over y, x, core).
Axes of the slice: x: 2, y: 2, z: 4, core: 2. Of those that a mesh axis runs over, the one named last changes fastest.
Arguments:
- saved: bfloat16 [4, 32, 4, 8, 384], P('section', 'dp'), may hold values from -6 to 6
- kernels: bfloat16 [4, 384, 3, 3, 384], P('section'), may hold values from -0.109375 to 0.109375
- head: bfloat16 [384, 512], replicated, may hold values from -0.3125 to 0.3125
- counts: int32 [8], P('dp'), may hold values from 1 to 4, as said below
- pairs: int32 [32], P('dp'), may hold values from 0 to 31, as said below
- valid: int32 [32], P('dp'), may hold values 0 or 1
Outputs:
- input_grads: bfloat16 [4, 32, 4, 8, 384], P('section', 'dp')
- weight_grads: float32 [4, 384, 3, 3, 384], P('section', 'dp')
- head_grad: float32 [384, 512], P('dp', 'section')
Inputs may be any that keep to these rules, and one draw needn't show every extreme that they name: Slot d * 4 + r holds a record exactly when r < counts[d]; at least one index of dp holds 4 records. pairs[pairs[i]] = i and pairs[i] != i.
All inputs are finite; a program needn't handle non-finite values. No bound on the sum of `valid` on one device may be relied on, other than what follows from the above.
Results may differ from a plain program's by a relative error of at most 0.012.
Values may be sent and summed in bfloat16 or wider, within the bound.
A program may use at most 64 MiB of HBM per device.

v0:
```python
import jax
import jax.numpy as jnp
from jax import lax
from jax.sharding import PartitionSpec as P

tau_value = 0.2
loss_scale = 32.0
norm_eps = 1e-06


def from_root(value, axis, source):
    kept = jnp.where(lax.axis_index(axis) == source, value, 0).astype(value.dtype)
    return lax.psum(kept, axis)


def passed_along(value, axis, steps):
    count = lax.axis_size(axis)
    initial, last = (max(0, -steps), min(count, count - steps))
    return lax.ppermute(value, axis, [(source, source + steps) for source in range(initial, last)])


def conv_apply(inputs, kernel):
    return lax.conv_general_dilated(
        inputs,
        kernel,
        (1, 1),
        "SAME",
        dimension_numbers=("NHWC", "IHWO", "NHWC"),
        preferred_element_type=jnp.float32,
    )


def conv_back(grads, kernel):
    return lax.conv_general_dilated(
        grads,
        jnp.flip(kernel, (1, 2)),
        (1, 1),
        "SAME",
        dimension_numbers=("NHWC", "OHWI", "NHWC"),
        preferred_element_type=jnp.float32,
    )


def kernel_grad(inputs, grads):
    return lax.conv_general_dilated(
        inputs,
        grads,
        (1, 1),
        ((1, 1), (1, 1)),
        dimension_numbers=("CHWN", "IHWO", "NHWC"),
        preferred_element_type=jnp.float32,
    )


def per_device(saved, kernels, head, counts, pairs, valid):
    inputs = saved[0]
    kernel = kernels[0]
    cap = inputs.shape[0]
    npos = inputs.shape[1] * inputs.shape[2]
    sections = lax.axis_size("section")
    section = lax.axis_index("section")
    rank = lax.axis_index("dp")
    slots = jnp.arange(cap, dtype=jnp.int32)
    mine = rank * cap + slots
    live = jnp.where((slots < counts[0]) & (valid == 1), 1.0, 0.0).astype(jnp.float32)
    live_b = live.astype(jnp.bfloat16)
    pre = conv_apply(inputs, kernel)
    sigma = jax.nn.sigmoid(pre)
    slope = sigma * (1.0 + pre * (1.0 - sigma))
    pooled = jnp.mean(inputs.astype(jnp.float32) + pre * sigma, axis=(1, 2)).astype(jnp.bfloat16)
    pooled = from_root(pooled, "section", sections - 1)
    proj = jnp.dot(pooled, head, preferred_element_type=jnp.float32)
    inv = lax.rsqrt(jnp.sum(proj * proj, axis=1, keepdims=True) + norm_eps)
    unit = proj * inv
    unit_b = unit.astype(jnp.bfloat16)

    def exp_scores(others):
        ids = jnp.arange(others.shape[0], dtype=jnp.int32)
        scores = (
            lax.dot_general(
                unit_b, others, (((1,), (1,)), ((), ())), preferred_element_type=jnp.float32
            )
            / tau_value
        )
        return (jnp.where(mine[:, None] != ids[None, :], jnp.exp(scores), 0.0), ids)

    start_sums = (jnp.zeros((cap,), jnp.float32), jnp.zeros((cap,), jnp.float32))
    others = lax.all_gather(unit_b, "dp", axis=0, tiled=True)
    flags = lax.all_gather(live_b, "dp", axis=0, tiled=True)
    expo, ids = exp_scores(others)
    flag_f = flags.astype(jnp.float32)
    total = start_sums[0] + jnp.sum(expo * flag_f[None, :], axis=1)
    mate = jnp.sum(jnp.where(pairs[:, None] == ids[None, :], flag_f[None, :], 0.0), axis=1)
    total, mate = (total, mate)
    share = live * mate
    coef = lax.optimization_barrier((share / total).astype(jnp.bfloat16))
    coef_own = coef.astype(jnp.float32)
    start_grad = jnp.zeros(unit.shape, jnp.float32)
    others = lax.all_gather(unit_b, "dp", axis=0, tiled=True)
    flags = lax.all_gather(live_b, "dp", axis=0, tiled=True)
    coefs = lax.all_gather(coef, "dp", axis=0, tiled=True)
    expo, ids = exp_scores(others)
    flag_f = flags.astype(jnp.float32)
    coef_f = coefs.astype(jnp.float32)
    mixing = expo * (
        coef_own[:, None] * flag_f[None, :] + coef_f[None, :] * live[:, None]
    ) - 2.0 * jnp.where(pairs[:, None] == ids[None, :], share[:, None], 0.0)
    dunit = start_grad + jnp.dot(
        mixing.astype(jnp.bfloat16), others, preferred_element_type=jnp.float32
    )
    dunit = dunit * (loss_scale / tau_value)
    along = jnp.sum(unit * dunit, axis=1, keepdims=True)
    dproj = ((dunit - unit * along) * inv).astype(jnp.bfloat16)
    col_width = head.shape[1] // sections
    dproj_cols = lax.dynamic_slice_in_dim(dproj, section * col_width, col_width, 1)
    head_term = lax.dot_general(
        pooled, dproj_cols, (((0,), (0,)), ((), ())), preferred_element_type=jnp.float32
    )
    head_grad = lax.psum_scatter(head_term, "dp", scatter_dimension=0, tiled=True)
    dpooled = lax.dot_general(
        dproj, head, (((1,), (1,)), ((), ())), preferred_element_type=jnp.float32
    ).astype(jnp.bfloat16)
    top = (dpooled.astype(jnp.float32) / npos).astype(jnp.bfloat16)
    cotan = jnp.broadcast_to(top[:, None, None, :], inputs.shape)

    def backward(cot_part, slope_part):
        dpre = (cot_part.astype(jnp.float32) * slope_part).astype(jnp.bfloat16)
        below = (cot_part.astype(jnp.float32) + conv_back(dpre, kernel)).astype(jnp.bfloat16)
        return (below, dpre)

    empty = jnp.zeros(inputs.shape, jnp.bfloat16)
    dx_out = empty
    du_out = empty
    for step in range(sections):
        active = section == sections - 1 - step
        dx_new, du_new = lax.cond(
            active, backward, lambda first, second: (empty, empty), cotan, slope
        )
        dx_out = jnp.where(active, dx_new, dx_out)
        du_out = jnp.where(active, du_new, du_out)
        if step + 1 < sections:
            arrived = passed_along(dx_new, "section", -1)
            cotan = jnp.where(section == sections - 2 - step, arrived, cotan)
    columns = lax.all_to_all(inputs, "dp", split_axis=3, concat_axis=0, tiled=True)
    start_w = jnp.zeros((columns.shape[3],) + kernel.shape[1:], jnp.float32)
    piece = lax.all_gather(du_out, "dp", axis=0, tiled=True)
    part = lax.slice_in_dim(columns, 0, piece.shape[0], axis=0)
    wgrad = start_w + kernel_grad(part, piece)
    return (dx_out[None], wgrad[None], head_grad)


def solution(mesh):
    return jax.shard_map(
        per_device,
        mesh=mesh,
        in_specs=(
            P("section", "dp", None, None, None),
            P("section", None, None, None, None),
            P(),
            P("dp"),
            P("dp"),
            P("dp"),
        ),
        out_specs=(
            P("section", "dp", None, None, None),
            P("section", "dp", None, None, None),
            P("dp", "section"),
        ),
        check_vma=False,
    )
```

profile of v0, /device:TPU:0, one launch (start us, length us, event | category | flops | bytes accessed | tf_op | source)
XLA Modules:
  0.0 129.6 jit_solution(12394622258385495259)
XLA Ops:
  7.2 0.0 copy-start
  7.2 0.0 copy-start.13
  7.2 2.8 %add_multiply_fusion = (f32[4,4,8,384]{3,0,2,1:T(4,128)S(1)}, f32[4,384]{1,0:T(4,128)S(1)}) fusion(bf16[1,4,4,8,384]{4,3,2,1,0:T(8,128)(2,1)} %param.14, bf16[1,384,3,3,384]{4,1,3,2,0:T(8,128)(2,1)} %param.15), kind=kOutput, calls=%fused_computation.27 | convolution fusion | flops 260061696 | bytes 2955264 | tf_op jit(solution)/shard_map/conv_general_dilated | solution.py:23
  10.0 0.0 copy-start.1
  10.1 13.5 %psum.7 = bf16[4,384]{1,0:T(4,128)(2,1)S(1)} all-reduce(bf16[4,384]{1,0:T(4,128)(2,1)S(1)} %fusion.17), channel_id=1, replica_groups=mesh['section'=4,'dp'=8] {'section'}, use_global_device_ids=true, to_apply=%region_1.2 | all-reduce | flops 1536 | bytes 6144 | tf_op jit(solution)/shard_map/psum | solution.py:13
  23.5 0.3 multiply_reduce_fusion.1
  23.8 0.1 fusion.32
  23.9 9.1 %all-gather = bf16[8,4,512]{2,1,0:T(4,128)(2,1)S(1)} all-gather(bf16[1,4,512]{2,1,0:T(4,128)(2,1)S(1)} %fusion.32), channel_id=1, replica_groups=mesh['section'=4,'dp'=8] {'dp'}, dimensions={0}, use_global_device_ids=true | all-gather | bytes 36864 | tf_op jit(solution)/shard_map/all_gather | solution.py:99
  33.7 0.6 dynamic-slice
  34.9 0.2 dynamic-update-slice
  35.2 13.2 %all-reduce = bf16[32]{0:T(256)(128)(2,1)S(1)} all-reduce(bf16[32]{0:T(256)(128)(2,1)S(1)} %dynamic-update-slice), channel_id=1, replica_groups=mesh['section'=4,'dp'=8] {'dp'}, use_global_device_ids=true, to_apply=%add | all-reduce | flops 32 | bytes 128
  48.4 0.0 copy-start.10
  48.4 0.3 multiply_reduce_fusion.2
  48.7 0.2 dynamic-update-slice.1
  49.0 11.8 %all-reduce.1 = bf16[32]{0:T(256)(128)(2,1)S(1)} all-reduce(bf16[32]{0:T(256)(128)(2,1)S(1)} %dynamic-update-slice.1), channel_id=1, replica_groups=mesh['section'=4,'dp'=8] {'dp'}, use_global_device_ids=true, to_apply=%add.1 | all-reduce | flops 32 | bytes 128
  60.8 0.3 multiply_reduce_fusion
  61.1 0.1 multiply_convert_fusion
  61.2 0.2 fusion.10
  61.4 0.1 conditional.4
  61.5 0.6 copy-done.6
  62.1 1.3 collective-permute-start
  63.4 1.3 %copy.48 = bf16[1,4,4,8,384]{3,2,1,4,0:T(4,128)(2,1)S(1)} copy(bf16[1,4,4,8,384]{4,3,2,1,0:T(8,128)(2,1)S(1)} %copy-done.10) | data formatting | bytes 196608 | tf_op jit(solution)/shard_map/squeeze | solution.py:56
  64.8 3.8 %collective-permute-done = bf16[4,4,8,384]{3,2,1,0:T(8,128)(2,1)S(1)} collective-permute-done((bf16[4,4,8,384]{3,2,1,0:T(8,128)(2,1)S(1)}, bf16[4,4,8,384]{3,2,1,0:T(8,128)(2,1)S(1)}, u32[]{:S(2)}, u32[]{:S(2)}) %collective-permute-start) | collective-permute-done | bytes 98336 | tf_op jit(solution)/shard_map/ppermute | solution.py:19
  68.7 0.7 conditional.5
  68.7 0.7 broadcast_in_dim.36.clone
  69.4 0.6 copy-done.8
  70.0 1.3 collective-permute-start.1
  71.3 0.5 bitcast_bitcast_fusion
  71.8 2.3 %reshape.36 = bf16[8,2,3072]{2,1,0:T(2,128)(2,1)} reshape(bf16[384,4,4,8]{3,2,1,0:T(4,128)(2,1)S(1)} %bitcast_bitcast_fusion) | data formatting | bytes 196608
  74.1 3.4 %all-to-all-start = ((bf16[8,2,3072]{2,1,0:T(2,128)(2,1)}), bf16[8,2,3072]{2,1,0:T(2,128)(2,1)S(1)}, u32[]{:S(2)}, u32[]{:S(2)}) async-start(bf16[8,2,3072]{2,1,0:T(2,128)(2,1)} %reshape.36), calls=%async_computation | async-start | bytes 196608 | tf_op jit(solution)/shard_map/all_to_all | solution.py:144
  77.5 0.0 reduce-scatter.2.cloned.1.call-start
  77.6 0.7 conditional.6
  77.6 0.7 broadcast_in_dim.41
  78.3 0.0 copy-start.2
  78.3 1.4 %collective-permute-start.2 = (bf16[4,4,8,384]{3,0,2,1:T(4,128)(2,1)}, bf16[4,4,8,384]{3,0,2,1:T(4,128)(2,1)S(1)}, u32[]{:S(2)}, u32[]{:S(2)}) collective-permute-start(bf16[4,4,8,384]{3,0,2,1:T(4,128)(2,1)} %get-tuple-element.57), channel_id=1, source_target_pairs={{8,0},{16,8},{24,16},{9,1},{17,9},{25,17},{10,2},{18,10},{26,18},{... | collective-permute-start | bytes 294920 | tf_op jit(solution)/shard_map/ppermute | solution.py:19
  79.8 0.9 fusion.18
  80.7 0.0 reduce-scatter.2.cloned.1.call-update
  80.7 1.9 %all-to-all-done = bf16[8,2,3072]{2,1,0:T(2,128)(2,1)S(1)} async-done(((bf16[8,2,3072]{2,1,0:T(2,128)(2,1)}), bf16[8,2,3072]{2,1,0:T(2,128)(2,1)S(1)}, u32[]{:S(2)}, u32[]{:S(2)}) %all-to-all-start) | async-done | bytes 98336 | tf_op jit(solution)/shard_map/all_to_all | solution.py:144
  82.6 1.8 %reshape.37 = bf16[384,4,4,8]{3,2,1,0:T(4,128)(2,1)S(1)} reshape(bf16[8,2,3072]{2,1,0:T(2,128)(2,1)S(1)} %all-to-all-done) | data formatting | bytes 196608
  84.4 2.3 %copy.42 = bf16[4,4,8,8,48]{4,0,3,2,1:T(4,128)(2,1)S(1)} copy(bf16[4,4,8,8,48]{2,1,0,4,3:T(4,128)(2,1)S(1)} %bitcast.45) | data formatting | bytes 196608 | tf_op jit(solution)/shard_map/all_to_all | solution.py:144
  86.8 5.4 %collective-permute-done.2 = bf16[4,4,8,384]{3,0,2,1:T(4,128)(2,1)S(1)} collective-permute-done((bf16[4,4,8,384]{3,0,2,1:T(4,128)(2,1)}, bf16[4,4,8,384]{3,0,2,1:T(4,128)(2,1)S(1)}, u32[]{:S(2)}, u32[]{:S(2)}) %collective-permute-start.2) | collective-permute-done | bytes 98336 | tf_op jit(solution)/shard_map/ppermute | solution.py:19
  92.1 3.0 %conditional.7 = (bf16[4,4,8,384]{3,2,1,0:T(8,128)(2,1)S(1)}, bf16[4,4,8,384]{3,2,1,0:T(8,128)(2,1)S(1)}) conditional(s32[]{:T(128)} %convert_element_type.94, () %tuple.40, (pred[]{:T(512)}, bf16[4,4,8,384]{3,0,2,1:T(4,128)(2,1)S(1)}, bf16[4,4,8,384]{3,2,1,0:T(8,128)(2,1)S(1)}, f32[4,4,8,384]{3,0,2,1:T(4,128)S(1)}, ...), branch_computations={%region_12.13_spmd, %region_13.14_spmd} | conditional | flops 259915776 | bytes 3932178 | solution.py:136
  92.1 0.1 fusion.7
  92.2 2.9 %fusion.6 = bf16[4,4,8,384]{3,0,2,1:T(4,128)(2,1)S(1)} fusion(bf16[4,4,8,384]{3,0,2,1:T(4,128)(2,1)S(1)} %fusion.7, bf16[384,3,3,384]{3,0,2,1:T(8,128)(2,1)} %get-tuple-element.43, bf16[4,4,8,384]{3,0,2,1:T(4,128)(2,1)S(1)} %get-tuple-element.40, bf16[4,4,8,384]{3,2,1,0:T(8,128)(2,1)S(1)} %get-tuple-element.91, pred[]{:T(512)} %get-tuple-element.39), kind=kOutput, calls=%fused_computation.13 | convolution fusion | flops 259719168 | bytes 3047425 | tf_op jit(solution)/shard_map/cond/branch_1_fun/conv_general_dilated | solution.py:34
  95.2 10.6 %all_gather.17 = bf16[32,4,8,384]{3,2,1,0:T(8,128)(2,1)S(1)} all-gather(bf16[4,4,8,384]{3,2,1,0:T(8,128)(2,1)S(1)} %select_select_fusion), channel_id=1, replica_groups=mesh['section'=4,'dp'=8] {'dp'}, dimensions={0}, use_global_device_ids=true | all-gather | bytes 884736 | tf_op jit(solution)/shard_map/all_gather | solution.py:146
  105.8 1.6 %convolution_bitcast_fusion = f32[1,48,3,3,384]{4,1,3,2,0:T(8,128)} fusion(bf16[32,4,8,48]{3,0,2,1:T(8,128)(2,1)S(1)} %bitcast.46, bf16[32,4,8,384]{3,2,1,0:T(8,128)(2,1)S(1)} %all_gather.17), kind=kOutput, calls=%fused_computation.17 | convolution fusion | flops 259522560 | bytes 1548288 | tf_op jit(solution)/shard_map/conv_general_dilated | solution.py:45
  107.4 0.7 select_bitcast_fusion
  108.1 14.6 %reduce-scatter.2.cloned.1.call-done = f32[48,128]{1,0:T(8,128)} async-done(((f32[384,128]{1,0:T(8,128)}), f32[48,128]{1,0:T(8,128)}) %reduce-scatter.2.cloned.1.call-update) | async-done | bytes 24592 | tf_op jit(solution)/shard_map/reduce_scatter | solution.py:119
  (44 shorter events, 0.3 us)
Async XLA Ops:
  7.2 16.4 %copy-start = (bf16[384,512]{1,0:T(8,128)(2,1)S(1)}, bf16[384,512]{1,0:T(8,128)(2,1)}, u32[]{:S(2)}) copy-start(bf16[384,512]{1,0:T(8,128)(2,1)} %param.16) | copy-start | bytes 1179652
  7.2 26.5 %copy-start.13 = (u32[32]{0:T(128)S(1)}, u32[32]{0:T(128)}, u32[]{:S(2)}) copy-start(u32[32]{0:T(128)} %constant.59) | copy-start | bytes 388
  7.2 26.4 %copy-start.11 = (s32[4]{0:T(128)S(1)}, s32[4]{0:T(128)}, u32[]{:S(2)}) copy-start(s32[4]{0:T(128)} %param.19) | copy-start | bytes 52
  7.2 41.2 %copy-start.12 = (s32[4]{0:T(128)S(1)}, s32[4]{0:T(128)}, u32[]{:S(2)}) copy-start(s32[4]{0:T(128)} %param.18) | copy-start | bytes 52
  10.0 58.6 %copy-start.1 = (f32[4,4,8,384]{3,0,2,1:T(4,128)}, f32[4,4,8,384]{3,0,2,1:T(4,128)S(1)}, u32[]{:S(2)}) copy-start(f32[4,4,8,384]{3,0,2,1:T(4,128)S(1)} %get-tuple-element.108) | copy-start | bytes 589828
  48.4 15.0 %copy-start.10 = (bf16[1,4,4,8,384]{4,3,2,1,0:T(8,128)(2,1)S(1)}, bf16[1,4,4,8,384]{4,3,2,1,0:T(8,128)(2,1)}, u32[]{:S(2)}) copy-start(bf16[1,4,4,8,384]{4,3,2,1,0:T(8,128)(2,1)} %param.14) | copy-start | bytes 294916
  61.5 0.6 copy-start.6
  62.1 2.7 %copy-start.4 = (bf16[4,4,8,384]{3,2,1,0:T(8,128)(2,1)}, bf16[4,4,8,384]{3,2,1,0:T(8,128)(2,1)S(1)}, u32[]{:S(2)}) copy-start(bf16[4,4,8,384]{3,2,1,0:T(8,128)(2,1)S(1)} %get-tuple-element.94) | copy-start | bytes 294916
  62.1 6.5 %collective-permute-start = (bf16[4,4,8,384]{3,2,1,0:T(8,128)(2,1)S(1)}, bf16[4,4,8,384]{3,2,1,0:T(8,128)(2,1)S(1)}, u32[]{:S(2)}, u32[]{:S(2)}) collective-permute-start(bf16[4,4,8,384]{3,2,1,0:T(8,128)(2,1)S(1)} %get-tuple-element.94), channel_id=1, source_target_pairs={{8,0},{16,8},{24,16},{9,1},{17,9},{25,17},{10,2},{18,10},{26,18},{... | collective-permute-start | bytes 294920 | tf_op jit(solution)/shard_map/ppermute | solution.py:19
  68.6 0.7 copy-start.3
  69.4 0.6 copy-start.8
  70.0 7.6 %collective-permute-start.1 = (bf16[4,4,8,384]{3,2,1,0:T(8,128)(2,1)}, bf16[4,4,8,384]{3,2,1,0:T(8,128)(2,1)}, u32[]{:S(2)}, u32[]{:S(2)}) collective-permute-start(bf16[4,4,8,384]{3,2,1,0:T(8,128)(2,1)} %get-tuple-element.96), channel_id=1, source_target_pairs={{8,0},{16,8},{24,16},{9,1},{17,9},{25,17},{10,2},{18,10},{26,18},{... | collective-permute-start | bytes 294920 | tf_op jit(solution)/shard_map/ppermute | solution.py:19
  74.1 8.5 %all-to-all-start = ((bf16[8,2,3072]{2,1,0:T(2,128)(2,1)}), bf16[8,2,3072]{2,1,0:T(2,128)(2,1)S(1)}, u32[]{:S(2)}, u32[]{:S(2)}) async-start(bf16[8,2,3072]{2,1,0:T(2,128)(2,1)} %reshape.36), calls=%async_computation | async-start | bytes 196608 | tf_op jit(solution)/shard_map/all_to_all | solution.py:144
  77.5 45.2 %reduce-scatter.2.cloned.1.call-start = ((), (), s32[]{:S(2)}) async-start(), calls=%async_computation.2 | async-start | bytes 221184 | tf_op jit(solution)/shard_map/reduce_scatter | solution.py:119
  78.3 13.8 %copy-start.2 = (f32[4,4,8,384]{3,0,2,1:T(4,128)S(1)}, f32[4,4,8,384]{3,0,2,1:T(4,128)}, u32[]{:S(2)}) copy-start(f32[4,4,8,384]{3,0,2,1:T(4,128)} %copy-done.1) | copy-start | bytes 589828
  78.3 13.8 %collective-permute-start.2 = (bf16[4,4,8,384]{3,0,2,1:T(4,128)(2,1)}, bf16[4,4,8,384]{3,0,2,1:T(4,128)(2,1)S(1)}, u32[]{:S(2)}, u32[]{:S(2)}) collective-permute-start(bf16[4,4,8,384]{3,0,2,1:T(4,128)(2,1)} %get-tuple-element.57), channel_id=1, source_target_pairs={{8,0},{16,8},{24,16},{9,1},{17,9},{25,17},{10,2},{18,10},{26,18},{... | collective-permute-start | bytes 294920 | tf_op jit(solution)/shard_map/ppermute | solution.py:19
  86.7 8.4 %copy-start.7 = (bf16[4,4,8,384]{3,2,1,0:T(8,128)(2,1)S(1)}, bf16[4,4,8,384]{3,2,1,0:T(8,128)(2,1)}, u32[]{:S(2)}) copy-start(bf16[4,4,8,384]{3,2,1,0:T(8,128)(2,1)} %copy-done.6) | copy-start | bytes 294916
  86.7 8.4 %copy-start.9 = (bf16[4,4,8,384]{3,2,1,0:T(8,128)(2,1)S(1)}, bf16[4,4,8,384]{3,2,1,0:T(8,128)(2,1)}, u32[]{:S(2)}) copy-start(bf16[4,4,8,384]{3,2,1,0:T(8,128)(2,1)} %copy-done.8) | copy-start | bytes 294916
  95.1 12.3 %copy-start.5 = (bf16[4,4,8,384]{3,2,1,0:T(8,128)(2,1)S(1)}, bf16[4,4,8,384]{3,2,1,0:T(8,128)(2,1)}, u32[]{:S(2)}) copy-start(bf16[4,4,8,384]{3,2,1,0:T(8,128)(2,1)} %copy-done.4) | copy-start | bytes 294916
Sparse Core Ops, SparseCore 0:
  81.9 40.7 reduce-scatter.1
where the time goes:
time: 130 us
  blocking collectives  58.1 us (45%)
  waiting for transfers between devices  25.8 us (20%)
  between operations  15.7 us (12%)
  local copies, waits for them, and re-layouts  12.1 us (9%)
  matrix products  9.3 us (7%)
  starting transfers between devices  7.38 us (6%)
    unnamed x2, blocking collectives  25 us
    reduce_scatter x1, waiting for transfers between devices, per_device(): lax.psum_scatter(head_term, 'dp', scatter_dimension=0, tiled=True)  14.6 us
    psum x1, blocking collectives, from_root(): return lax.psum(kept, axis)  13.5 us
    all_gather x1, blocking collectives, per_device(): piece = lax.all_gather(du_out, 'dp', axis=0, tiled=True)  10.6 us
    ppermute x3, waiting for transfers between devices, passed_along(): lax.ppermute(value, axis, [(source, source + steps) for source in range(i...  9.21 us
    all_gather x1, blocking collectives, per_device(): others = lax.all_gather(unit_b, 'dp', axis=0, tiled=True)  9.08 us
    unnamed x37, local copies, waits for them, and re-layouts  7.06 us
    ppermute x3, starting transfers between devices, passed_along(): lax.ppermute(value, axis, [(source, source + steps) for source in range(i...  3.98 us
  transfers between devices with their start and end apart: 5, of which 4 were waited for; matrix products, arithmetic and copies ran while one was open for 12% of the time, Pallas kernels for 0%

commit v1 on v0

v1 whole, which is shorter than its diff:
```python
import functools

import jax
import jax.numpy as jnp
from jax import lax
from jax.experimental import pallas as pl
from jax.experimental.pallas import tpu as pltpu
from jax.sharding import PartitionSpec as P

TAU = 0.2
LOSS_SCALE = 32.0
EPS = 1e-06
MESH = pl.DeviceIdType.MESH
F32 = jnp.float32
BF16 = jnp.bfloat16


def dot(a, b, ca, cb):
    return lax.dot_general(a, b, (((ca,), (cb,)), ((), ())), preferred_element_type=F32)


def fill_patches(dst_ref, v, dims, flip):
    recs, ph, pw = dims
    rows, ch = v.shape
    w = lax.broadcasted_iota(jnp.int32, (rows, ch), 0) % pw
    for j in range(3):
        if j == 1:
            vj = v
        elif j == 0:
            vj = jnp.where(w > 0, pltpu.roll(v, 1, 0), 0.0)
        else:
            vj = jnp.where(w < pw - 1, pltpu.roll(v, rows - 1, 0), 0.0)
        cells = vj.reshape(recs, ph, pw, ch)
        edge = jnp.zeros((recs, 1, pw, ch), F32)
        for i in range(3):
            if i == 1:
                vij = cells
            elif i == 0:
                vij = jnp.concatenate([edge, cells[:, : ph - 1]], axis=1)
            else:
                vij = jnp.concatenate([cells[:, 1:], edge], axis=1)
            tap = 3 * i + j
            if flip:
                tap = 8 - tap
            dst_ref[:, tap * ch : (tap + 1) * ch] = vij.reshape(rows, ch).astype(BF16)


def body(cfg, x_ref, k_hbm, head_ref, counts_ref, pairs_ref, valid_ref,
         dx_ref, wg_ref, hg_ref,
         k_ref, kt_ref, patch_ref, slope_ref, pooled_ref, g_ref, dproj_ref, pt_ref,
         hgs_ref, hgr_ref, xt_ref, xg_ref, lhs_ref, dg_ref, acc_ref, cot_ref, relay_ref, out_ref,
         k_sem, gs_sem, gr_sem, hs_sem, hr_sem, xs_sem, xr_sem, ds_sem, dr_sem, cs_sem, cr_sem):
    S, D, cap, ph, pw, ch, emb, cw, cp = cfg
    rows = cap * ph * pw
    sec = lax.axis_index("section")
    rank = lax.axis_index("dp")
    last = S - 1

    def peer(off):
        return lax.rem(rank + off, D)

    def source(off):
        return lax.rem(rank + D - off, D)

    k_copies = []
    for i in range(3):
        cpy = pltpu.make_async_copy(k_hbm.at[3 * i : 3 * i + 3], k_ref.at[3 * i : 3 * i + 3], k_sem.at[i])
        cpy.start()
        k_copies.append(cpy)

    barrier = pltpu.get_barrier_semaphore()
    for off in range(1, D):
        pl.semaphore_signal(barrier, inc=1, device_id=(sec, peer(off)), device_id_type=MESH)
    for off in range(1, S):
        pl.semaphore_signal(barrier, inc=1, device_id=(lax.rem(sec + off, S), rank), device_id_type=MESH)

    x = x_ref[0].astype(F32).reshape(rows, ch)
    fill_patches(patch_ref, x, (cap, ph, pw), False)
    pre = None
    for i in range(3):
        k_copies[i].wait()
        kk = k_ref[3 * i : 3 * i + 3].reshape(3 * ch, ch)
        term = dot(patch_ref[:, 3 * i * ch : 3 * (i + 1) * ch], kk, 1, 0)
        pre = term if pre is None else pre + term
    sig = 1.0 / (1.0 + jnp.exp(-pre))
    slope_ref[...] = sig * (1.0 + pre * (1.0 - sig))

    pl.semaphore_wait(barrier, D - 1 + S - 1)

    def pooled_copy(off):
        return pltpu.make_async_remote_copy(
            src_ref=g_ref.at[rank], dst_ref=g_ref.at[rank],
            send_sem=gs_sem.at[off - 1], recv_sem=gr_sem.at[off - 1],
            device_id=(sec, peer(off)), device_id_type=MESH)

    @pl.when(sec == last)
    def _():
        y = x + pre * sig
        mean = jnp.sum(y.reshape(cap, ph * pw, ch), axis=1) * (1.0 / (ph * pw))
        mean = mean.astype(BF16).astype(F32)
        pooled_ref[...] = jnp.zeros(pooled_ref.shape, F32)
        pooled_ref[0:cap, :ch] = mean
        row = lax.broadcasted_iota(jnp.int32, (8, 128), 0)
        lane = lax.broadcasted_iota(jnp.int32, (8, 128), 1)
        meta = jnp.where(lane == 1, -1.0, 0.0)
        for r in range(cap):
            live = jnp.where((r < counts_ref[0]) & (valid_ref[r] == 1), 1.0, 0.0)
            p = pairs_ref[r]
            pid = ((p // cap) * 8 + p % cap).astype(F32)
            meta = jnp.where((row == r) & (lane == 0), live, meta)
            meta = jnp.where((row == r) & (lane == 1), pid, meta)
        pooled_ref[:, ch:] = meta
        g_ref[rank] = pooled_ref[...]
        for off in range(1, D):
            pooled_copy(off).start()

    def x_copy(off):
        return pltpu.make_async_remote_copy(
            src_ref=xt_ref.at[peer(off)], dst_ref=xg_ref.at[rank],
            send_sem=xs_sem.at[off - 1], recv_sem=xr_sem.at[off - 1],
            device_id=(sec, peer(off)), device_id_type=MESH)

    xt = x.T
    for p in range(D):
        blk = xt[p * cw : (p + 1) * cw]
        if cp != cw:
            blk = jnp.concatenate([blk, jnp.zeros((cp - cw, rows), F32)], axis=0)
        xt_ref[p] = blk.astype(BF16)
    xg_ref[rank] = xt_ref[rank]
    for off in range(1, D):
        x_copy(off).start()

    for t in range(9):
        kt_ref[t * ch : (t + 1) * ch, :] = k_ref[t].T

    ew = emb // S

    def head_copy(off):
        to = lax.rem(sec + off, S)
        return pltpu.make_async_remote_copy(
            src_ref=hgs_ref.at[to], dst_ref=hgr_ref,
            send_sem=hs_sem.at[off - 1], recv_sem=hr_sem.at[0],
            device_id=(to, rank), device_id_type=MESH)

    @pl.when(sec == last)
    def _():
        for off in range(1, D):
            pooled_copy(off).wait()
        n = D * 8
        g = g_ref[...].reshape(n, ch + 128)
        pooled = g[:, :ch].astype(BF16)
        meta = g[:, ch:]
        meta_t = meta.T
        live_col, pair_col = meta[:, 0:1], meta[:, 1:2]
        live_row, pair_row = meta_t[0:1, :], meta_t[1:2, :]
        ii = lax.broadcasted_iota(jnp.int32, (n, n), 0)
        jj = lax.broadcasted_iota(jnp.int32, (n, n), 1)
        head = head_ref[...]
        proj = dot(pooled, head, 1, 0)
        inv = lax.rsqrt(jnp.sum(proj * proj, axis=1, keepdims=True) + EPS)
        unit = proj * inv
        unit_b = unit.astype(BF16)
        scores = dot(unit_b, unit_b, 1, 1) / TAU
        expo = jnp.where(ii != jj, jnp.exp(scores), 0.0)
        is_mate = pair_col == jj.astype(F32)
        is_mate_t = pair_row == ii.astype(F32)
        total_col = jnp.sum(expo * live_row, axis=1, keepdims=True)
        total_row = jnp.sum(expo * live_col, axis=0, keepdims=True)
        share_col = live_col * jnp.sum(jnp.where(is_mate, live_row, 0.0), axis=1, keepdims=True)
        share_row = live_row * jnp.sum(jnp.where(is_mate_t, live_col, 0.0), axis=0, keepdims=True)
        coef_col = (share_col / total_col).astype(BF16).astype(F32)
        coef_row = (share_row / total_row).astype(BF16).astype(F32)
        mixing = expo * (coef_col * live_row + coef_row * live_col) - 2.0 * jnp.where(is_mate, share_col, 0.0)
        dunit = dot(mixing.astype(BF16), unit_b, 1, 0) * (LOSS_SCALE / TAU)
        along = jnp.sum(unit * dunit, axis=1, keepdims=True)
        dproj = ((dunit - unit * along) * inv).astype(BF16)
        dproj_ref[...] = dproj.astype(F32)
        mine = dproj_ref[pl.ds(pl.multiple_of(rank * 8, 8), 8), :].astype(BF16)
        dpooled = dot(mine, head, 1, 1).astype(BF16)
        top = (dpooled.astype(F32) / (ph * pw)).astype(BF16).astype(F32)
        for r in range(cap):
            cot_ref[r * ph * pw : (r + 1) * ph * pw, :] = jnp.broadcast_to(top[r : r + 1], (ph * pw, ch))

    def relay_copy():
        return pltpu.make_async_remote_copy(
            src_ref=out_ref, dst_ref=relay_ref,
            send_sem=cs_sem.at[0], recv_sem=cr_sem.at[0],
            device_id=(lax.rem(sec + S - 1, S), rank), device_id_type=MESH)

    def build_lhs():
        for off in range(1, D):
            x_copy(off).wait()
        lane = lax.broadcasted_iota(jnp.int32, (cp, rows), 1)
        w = lane % pw
        h = (lane // pw) % ph

        def one(d, carry):
            xd = xg_ref[d].astype(F32)
            for i in range(3):
                for j in range(3):
                    s = (i - 1) * pw + (j - 1)
                    v = xd if s == 0 else pltpu.roll(xd, (-s) % rows, 1)
                    ok = (h + (i - 1) >= 0) & (h + (i - 1) < ph) & (w + (j - 1) >= 0) & (w + (j - 1) < pw)
                    t = 3 * i + j
                    lhs_ref[d, t * cp : (t + 1) * cp, :] = jnp.where(ok, v, 0.0).astype(BF16)
            return carry

        lax.fori_loop(0, D, one, 0)

    @pl.when(sec != last)
    def _():
        build_lhs()
        relay_copy().wait_recv()
        cot_ref[...] = relay_ref[...].astype(F32)

    def d_copy(off):
        return pltpu.make_async_remote_copy(
            src_ref=dg_ref.at[rank], dst_ref=dg_ref.at[rank],
            send_sem=ds_sem.at[off - 1], recv_sem=dr_sem.at[off - 1],
            device_id=(sec, peer(off)), device_id_type=MESH)

    cot = cot_ref[...]
    dpre = (cot * slope_ref[...]).astype(BF16)
    dg_ref[rank] = dpre

    @pl.when(sec == 0)
    def _():
        for off in range(1, D):
            d_copy(off).start()

    fill_patches(patch_ref, dpre.astype(F32), (cap, ph, pw), True)
    below = cot_ref[...] + dot(patch_ref[...], kt_ref[...], 1, 0)
    out_ref[...] = below.astype(BF16)
    dx_ref[0] = below.reshape(cap, ph, pw, ch).astype(BF16)

    @pl.when(sec > 0)
    def _():
        relay_copy().start()
        for off in range(1, D):
            d_copy(off).start()

    @pl.when(sec == last)
    def _():
        build_lhs()
        n = D * 8
        g = g_ref[...].reshape(n, ch + 128)
        pt = g[:, :ch].T
        for p in range(D):
            pt_ref[p, 0:cw] = pt[p * cw : (p + 1) * cw]
        own = pt_ref[rank].astype(BF16)
        hg = dot(own, dproj_ref[...].astype(BF16), 1, 0)
        for s in range(S):
            hgs_ref[s] = hg[:, s * ew : (s + 1) * ew]
        for off in range(1, S):
            head_copy(off).start()

    acc_ref[...] = dot(lhs_ref[rank], dg_ref[rank], 1, 0)

    def gather_step(off, carry):
        d_copy(off).wait()
        d = source(off)
        acc_ref[...] += dot(lhs_ref[d], dg_ref[d], 1, 0)
        return carry

    lax.fori_loop(1, D, gather_step, 0)
    for t in range(9):
        wg_ref[t] = acc_ref[t * cp : t * cp + cw, :]

    @pl.when(sec == last)
    def _():
        hg_ref[...] = hgs_ref[last, 0:cw, :]
        for off in range(1, S):
            head_copy(off).wait_send()

    @pl.when(sec != last)
    def _():
        head_copy(1).wait_recv()
        hg_ref[...] = hgr_ref[0:cw, :]

    @pl.when(sec > 0)
    def _():
        relay_copy().wait_send()


def per_device(mesh_sizes, saved, kernels, head, counts, pairs, valid):
    S, D = mesh_sizes
    _, cap, ph, pw, ch = saved.shape
    emb = head.shape[1]
    cw = ch // D
    cp = -(-cw // 16) * 16
    rows = cap * ph * pw
    taps = jnp.transpose(kernels[0], (1, 2, 0, 3)).reshape(9, ch, ch)
    cfg = (S, D, cap, ph, pw, ch, emb, cw, cp)
    vmem = pl.BlockSpec(memory_space=pltpu.VMEM)
    smem = pl.BlockSpec(memory_space=pltpu.SMEM)
    sem = pltpu.SemaphoreType.DMA
    dx, wg, hg = pl.pallas_call(
        functools.partial(body, cfg),
        out_shape=(
            jax.ShapeDtypeStruct((1, cap, ph, pw, ch), BF16),
            jax.ShapeDtypeStruct((9, cw, ch), F32),
            jax.ShapeDtypeStruct((cw, emb // S), F32),
        ),
        in_specs=[vmem, pl.BlockSpec(memory_space=pl.ANY), vmem, smem, smem, smem],
        out_specs=(vmem, vmem, vmem),
        scratch_shapes=[
            pltpu.VMEM((9, ch, ch), BF16),
            pltpu.VMEM((9 * ch, ch), BF16),
            pltpu.VMEM((rows, 9 * ch), BF16),
            pltpu.VMEM((rows, ch), F32),
            pltpu.VMEM((8, ch + 128), F32),
            pltpu.VMEM((D, 8, ch + 128), F32),
            pltpu.VMEM((D * 8, emb), F32),
            pltpu.VMEM((D, cp, D * 8), F32),
            pltpu.VMEM((S, cp, emb // S), F32),
            pltpu.VMEM((cp, emb // S), F32),
            pltpu.VMEM((D, cp, rows), BF16),
            pltpu.VMEM((D, cp, rows), BF16),
            pltpu.VMEM((D, 9 * cp, rows), BF16),
            pltpu.VMEM((D, rows, ch), BF16),
            pltpu.VMEM((9 * cp, ch), F32),
            pltpu.VMEM((rows, ch), F32),
            pltpu.VMEM((rows, ch), BF16),
            pltpu.VMEM((rows, ch), BF16),
            sem((3,)),
            sem((D - 1,)), sem((D - 1,)),
            sem((S - 1,)), sem((1,)),
            sem((D - 1,)), sem((D - 1,)),
            sem((D - 1,)), sem((D - 1,)),
            sem((1,)), sem((1,)),
        ],
        compiler_params=pltpu.CompilerParams(
            collective_id=0, has_side_effects=True, vmem_limit_bytes=50 * 2**20
        ),
    )(saved, taps, head, counts, pairs, valid)
    wgrad = jnp.transpose(wg.reshape(3, 3, cw, ch), (2, 0, 1, 3))
    return dx, wgrad[None], hg


def solution(mesh):
    sizes = (mesh.shape["section"], mesh.shape["dp"])
    return jax.shard_map(
        functools.partial(per_device, sizes),
        mesh=mesh,
        in_specs=(
            P("section", "dp", None, None, None),
            P("section", None, None, None, None),
            P(),
            P("dp"),
            P("dp"),
            P("dp"),
        ),
        out_specs=(
            P("section", "dp", None, None, None),
            P("section", "dp", None, None, None),
            P("dp", "section"),
        ),
        check_vma=False,
    )
```

time: 130 us -> 43.2 us (0.33)
  the two profiles are of different devices: /device:TPU:0 before, /device:TPU:1 now
where the time goes in v1:
time: 43.2 us; the launch traced here: 42.9 us
  Pallas kernels  34.6 us (80%)
  local copies, waits for them, and re-layouts  7.03 us (16%)
  between operations  1.3 us (3%)
    pallas_call x1, Pallas kernels, per_device(): pl.pallas_call(functools.partial(body, cfg), out_shape=(jax.ShapeDtypeStr...  34.6 us
    unnamed x13, local copies, waits for them, and re-layouts  7.03 us

profile of v1, /device:TPU:1, one launch (start us, length us, event | category | flops | bytes accessed | tf_op | source)
XLA Modules:
  0.0 42.9 jit_solution(6325613787597365489)
XLA Ops:
  1.3 0.0 copy-start
  1.3 1.7 %copy-done = bf16[1,384,3,3,384]{4,1,3,2,0:T(8,128)(2,1)S(1)} copy-done((bf16[1,384,3,3,384]{4,1,3,2,0:T(8,128)(2,1)S(1)}, bf16[1,384,3,3,384]{4,1,3,2,0:T(8,128)(2,1)}, u32[]{:S(2)}) %copy-start) | copy-done | bytes 2654232
  3.0 0.0 copy-start.1
  3.0 1.0 %copy-done.1 = bf16[384,512]{1,0:T(8,128)(2,1)S(1)} copy-done((bf16[384,512]{1,0:T(8,128)(2,1)S(1)}, bf16[384,512]{1,0:T(8,128)(2,1)}, u32[]{:S(2)}) %copy-start.1) | copy-done | bytes 393240
  4.0 0.0 copy-start.2
  4.0 0.9 %copy-done.2 = bf16[1,4,4,8,384]{4,3,2,1,0:T(8,128)(2,1)S(1)} copy-done((bf16[1,4,4,8,384]{4,3,2,1,0:T(8,128)(2,1)S(1)}, bf16[1,4,4,8,384]{4,3,2,1,0:T(8,128)(2,1)}, u32[]{:S(2)}) %copy-start.2) | copy-done | bytes 98328
  4.9 0.0 copy-start.3
  4.9 0.7 %copy-done.3 = s32[4]{0:T(128)S(1)} copy-done((s32[4]{0:T(128)S(1)}, s32[4]{0:T(128)}, u32[]{:S(2)}) %copy-start.3) | copy-done | bytes 40
  5.6 0.0 copy-start.4
  5.6 0.7 %copy-done.4 = s32[4]{0:T(128)S(1)} copy-done((s32[4]{0:T(128)S(1)}, s32[4]{0:T(128)}, u32[]{:S(2)}) %copy-start.4) | copy-done | bytes 40
  6.2 34.6 %shard_map.85 = (bf16[1,4,4,8,384]{4,3,2,1,0:T(8,128)(2,1)S(1)}, f32[9,48,384]{2,1,0:T(8,128)S(1)}, f32[48,128]{1,0:T(8,128)S(1)}) custom-call(bf16[1,4,4,8,384]{4,3,2,1,0:T(8,128)(2,1)S(1)} %copy-done.2, bf16[9,384,384]{2,1,0:T(8,128)(2,1)S(1)} %bitcast.10, bf16[384,512]{1,0:T(8,128)(2,1)S(1)} %copy-done.1, s32[1]{0:T(128)S(6)} %copy.12.counts_ref, ...), custom_call_target="tpu_custom_call" | custom-call | tf_op jit(solution)/shard_map/pallas_call | solution.py:297
  40.8 0.6 %copy.13 = bf16[1,4,4,8,384]{4,3,2,1,0:T(8,128)(2,1)} copy(bf16[1,4,4,8,384]{4,3,2,1,0:T(8,128)(2,1)S(1)} %get-tuple-element.12) | data formatting | bytes 196608
  41.5 0.8 %copy.14 = f32[1,48,3,3,384]{4,1,3,2,0:T(8,128)} copy(f32[1,48,3,3,384]{4,1,3,2,0:T(8,128)S(1)} %bitcast.11) | data formatting | bytes 1327104
  42.3 0.6 %copy.15 = f32[48,128]{1,0:T(8,128)} copy(f32[48,128]{1,0:T(8,128)S(1)} %get-tuple-element.14) | data formatting | bytes 49152
Async XLA Ops:
  1.3 1.8 %copy-start = (bf16[1,384,3,3,384]{4,1,3,2,0:T(8,128)(2,1)S(1)}, bf16[1,384,3,3,384]{4,1,3,2,0:T(8,128)(2,1)}, u32[]{:S(2)}) copy-start(bf16[1,384,3,3,384]{4,1,3,2,0:T(8,128)(2,1)} %param.7) | copy-start | bytes 7962628
  3.0 1.0 %copy-start.1 = (bf16[384,512]{1,0:T(8,128)(2,1)S(1)}, bf16[384,512]{1,0:T(8,128)(2,1)}, u32[]{:S(2)}) copy-start(bf16[384,512]{1,0:T(8,128)(2,1)} %head_ref.1) | copy-start | bytes 1179652
  4.0 0.9 %copy-start.2 = (bf16[1,4,4,8,384]{4,3,2,1,0:T(8,128)(2,1)S(1)}, bf16[1,4,4,8,384]{4,3,2,1,0:T(8,128)(2,1)}, u32[]{:S(2)}) copy-start(bf16[1,4,4,8,384]{4,3,2,1,0:T(8,128)(2,1)} %x_ref.1) | copy-start | bytes 294916
  4.9 0.7 %copy-start.3 = (s32[4]{0:T(128)S(1)}, s32[4]{0:T(128)}, u32[]{:S(2)}) copy-start(s32[4]{0:T(128)} %pairs_ref.1) | copy-start | bytes 52
  5.6 0.7 %copy-start.4 = (s32[4]{0:T(128)S(1)}, s32[4]{0:T(128)}, u32[]{:S(2)}) copy-start(s32[4]{0:T(128)} %valid_ref.1) | copy-start | bytes 52

commit v2 on v1

--- a/solution.py
+++ b/solution.py
@@ -13,6 +13,7 @@
 MESH = pl.DeviceIdType.MESH
 F32 = jnp.float32
 BF16 = jnp.bfloat16
+HBM = pltpu.HBM
 
 
 def dot(a, b, ca, cb):
@@ -45,28 +46,51 @@
             dst_ref[:, tap * ch : (tap + 1) * ch] = vij.reshape(rows, ch).astype(BF16)
 
 
-def body(cfg, x_ref, k_hbm, head_ref, counts_ref, pairs_ref, valid_ref,
-         dx_ref, wg_ref, hg_ref,
-         k_ref, kt_ref, patch_ref, slope_ref, pooled_ref, g_ref, dproj_ref, pt_ref,
-         hgs_ref, hgr_ref, xt_ref, xg_ref, lhs_ref, dg_ref, acc_ref, cot_ref, relay_ref, out_ref,
-         k_sem, gs_sem, gr_sem, hs_sem, hr_sem, xs_sem, xr_sem, ds_sem, dr_sem, cs_sem, cr_sem):
-    S, D, cap, ph, pw, ch, emb, cw, cp = cfg
+def body(cfg, x_hbm, k_hbm, head_hbm, counts_hbm, pairs_hbm, valid_hbm,
+         dx_hbm, wg_hbm, hg_hbm, dx_ref, wg_ref, hg_ref, out_sem,
+         x_ref, head_ref, counts_ref, pairs_ref, valid_ref,
+         k_ref, kt0_ref, kt1_ref, patch_ref, patch0_ref, patch1_ref, part_ref, slope_ref,
+         pooled_ref, g_ref, dproj_ref, pt_ref,
+         hgs_ref, hgr_ref, xt_ref, xg_ref, lhs_ref, dg0_ref, dg1_ref, acc0_ref, acc1_ref,
+         top_ref, relay0_ref, relay1_ref, out0_ref, out1_ref,
+         in_sem, k_sem, gs_sem, gr_sem, hs_sem, hr_sem, xs_sem, xr_sem,
+         ds_sem, dr_sem, fs_sem, fr_sem, cs_sem, cr_sem):
+    S, D, cap, ph, pw, ch, emb, cw, cp, c0 = cfg
+    C = D // 2
     rows = cap * ph * pw
+    cells = ph * pw
     sec = lax.axis_index("section")
     rank = lax.axis_index("dp")
+    chip = rank // 2
+    core = rank % 2
+    partner = chip * 2 + 1 - core
     last = S - 1
+    span = ((0, c0), (c0, ch))
+    dg = (dg0_ref, dg1_ref)
+    acc = (acc0_ref, acc1_ref)
+    relay = (relay0_ref, relay1_ref)
+    out = (out0_ref, out1_ref)
+    patches = (patch0_ref, patch1_ref)
+    kt = (kt0_ref, kt1_ref)
 
     def peer(off):
         return lax.rem(rank + off, D)
 
-    def source(off):
-        return lax.rem(rank + D - off, D)
-
+    x_in = pltpu.make_async_copy(x_hbm, x_ref, in_sem.at[0])
+    x_in.start()
     k_copies = []
     for i in range(3):
         cpy = pltpu.make_async_copy(k_hbm.at[3 * i : 3 * i + 3], k_ref.at[3 * i : 3 * i + 3], k_sem.at[i])
         cpy.start()
         k_copies.append(cpy)
+    small = [
+        pltpu.make_async_copy(counts_hbm, counts_ref, in_sem.at[1]),
+        pltpu.make_async_copy(pairs_hbm, pairs_ref, in_sem.at[2]),
+        pltpu.make_async_copy(valid_hbm, valid_ref, in_sem.at[3]),
+        pltpu.make_async_copy(head_hbm, head_ref, in_sem.at[4]),
+    ]
+    for cpy in small:
+        cpy.start()
 
     barrier = pltpu.get_barrier_semaphore()
     for off in range(1, D):
@@ -74,6 +98,7 @@
     for off in range(1, S):
         pl.semaphore_signal(barrier, inc=1, device_id=(lax.rem(sec + off, S), rank), device_id_type=MESH)
 
+    x_in.wait()
     x = x_ref[0].astype(F32).reshape(rows, ch)
     fill_patches(patch_ref, x, (cap, ph, pw), False)
     pre = None
@@ -84,6 +109,8 @@
         pre = term if pre is None else pre + term
     sig = 1.0 / (1.0 + jnp.exp(-pre))
     slope_ref[...] = sig * (1.0 + pre * (1.0 - sig))
+    for cpy in small:
+        cpy.wait()
 
     pl.semaphore_wait(barrier, D - 1 + S - 1)
 
@@ -96,7 +123,7 @@
     @pl.when(sec == last)
     def _():
         y = x + pre * sig
-        mean = jnp.sum(y.reshape(cap, ph * pw, ch), axis=1) * (1.0 / (ph * pw))
+        mean = jnp.sum(y.reshape(cap, cells, ch), axis=1) * (1.0 / cells)
         mean = mean.astype(BF16).astype(F32)
         pooled_ref[...] = jnp.zeros(pooled_ref.shape, F32)
         pooled_ref[0:cap, :ch] = mean
@@ -131,7 +158,9 @@
         x_copy(off).start()
 
     for t in range(9):
-        kt_ref[t * ch : (t + 1) * ch, :] = k_ref[t].T
+        kt_t = k_ref[t].T
+        kt0_ref[t * c0 : (t + 1) * c0, :] = kt_t[:c0]
+        kt1_ref[t * (ch - c0) : (t + 1) * (ch - c0), :] = kt_t[c0:]
 
     ew = emb // S
 
@@ -177,14 +206,16 @@
         dproj_ref[...] = dproj.astype(F32)
         mine = dproj_ref[pl.ds(pl.multiple_of(rank * 8, 8), 8), :].astype(BF16)
         dpooled = dot(mine, head, 1, 1).astype(BF16)
-        top = (dpooled.astype(F32) / (ph * pw)).astype(BF16).astype(F32)
-        for r in range(cap):
-            cot_ref[r * ph * pw : (r + 1) * ph * pw, :] = jnp.broadcast_to(top[r : r + 1], (ph * pw, ch))
-
-    def relay_copy():
-        return pltpu.make_async_remote_copy(
-            src_ref=out_ref, dst_ref=relay_ref,
-            send_sem=cs_sem.at[0], recv_sem=cr_sem.at[0],
+        top = (dpooled.astype(F32) / cells).astype(BF16).astype(F32)
+        for q, (lo, hi) in enumerate(span):
+            for r in range(cap):
+                relay[q][r * cells : (r + 1) * cells, :] = jnp.broadcast_to(
+                    top[r : r + 1, lo:hi], (cells, hi - lo)).astype(BF16)
+
+    def relay_copy(q):
+        return pltpu.make_async_remote_copy(
+            src_ref=out[q], dst_ref=relay[q],
+            send_sem=cs_sem.at[q], recv_sem=cr_sem.at[q],
             device_id=(lax.rem(sec + S - 1, S), rank), device_id_type=MESH)
 
     def build_lhs():
@@ -210,34 +241,70 @@
     @pl.when(sec != last)
     def _():
         build_lhs()
-        relay_copy().wait_recv()
-        cot_ref[...] = relay_ref[...].astype(F32)
-
-    def d_copy(off):
-        return pltpu.make_async_remote_copy(
-            src_ref=dg_ref.at[rank], dst_ref=dg_ref.at[rank],
-            send_sem=ds_sem.at[off - 1], recv_sem=dr_sem.at[off - 1],
-            device_id=(sec, peer(off)), device_id_type=MESH)
-
-    cot = cot_ref[...]
-    dpre = (cot * slope_ref[...]).astype(BF16)
-    dg_ref[rank] = dpre
-
-    @pl.when(sec == 0)
-    def _():
-        for off in range(1, D):
-            d_copy(off).start()
-
-    fill_patches(patch_ref, dpre.astype(F32), (cap, ph, pw), True)
-    below = cot_ref[...] + dot(patch_ref[...], kt_ref[...], 1, 0)
-    out_ref[...] = below.astype(BF16)
-    dx_ref[0] = below.reshape(cap, ph, pw, ch).astype(BF16)
+
+    def near_copy(q):
+        return pltpu.make_async_remote_copy(
+            src_ref=dg[q].at[rank], dst_ref=dg[q].at[rank],
+            send_sem=ds_sem.at[q, 0], recv_sem=dr_sem.at[q, 0],
+            device_id=(sec, partner), device_id_type=MESH)
+
+    def far_copy(q, off):
+        return pltpu.make_async_remote_copy(
+            src_ref=dg[q].at[rank], dst_ref=dg[q].at[rank],
+            send_sem=ds_sem.at[q, off], recv_sem=dr_sem.at[q, off],
+            device_id=(sec, lax.rem(chip + off, C) * 2 + core), device_id_type=MESH)
+
+    def far_source(off):
+        return lax.rem(chip + C - off, C) * 2
+
+    def forward(q, off):
+        d = far_source(off) + core
+        return pltpu.make_async_remote_copy(
+            src_ref=dg[q].at[d], dst_ref=dg[q].at[d],
+            send_sem=fs_sem.at[q, off - 1], recv_sem=fr_sem.at[q, off - 1],
+            device_id=(sec, partner), device_id_type=MESH)
+
+    def start_gather(q):
+        for off in range(1, C):
+            far_copy(q, off).start()
+        near_copy(q).start()
+
+    cots = []
+    for q, (lo, hi) in enumerate(span):
+        @pl.when(sec != last)
+        def _():
+            relay_copy(q).wait_recv()
+
+        cot = relay[q][...].astype(F32)
+        dpre = (cot * slope_ref[:, lo:hi]).astype(BF16)
+        dg[q][rank] = dpre
+
+        @pl.when(sec == 0)
+        def _():
+            start_gather(q)
+
+        fill_patches(patches[q], dpre.astype(F32), (cap, ph, pw), True)
+        if q == 0:
+            part_ref[...] = dot(patches[0][...], kt[0][...], 1, 0)
+
+    for q, (lo, hi) in enumerate(span):
+        below = relay[q][...].astype(F32) + (
+            part_ref[:, lo:hi] + dot(patches[1][...], kt[1][:, lo:hi], 1, 0))
+        out[q][...] = below.astype(BF16)
+
+        @pl.when(sec > 0)
+        def _():
+            relay_copy(q).start()
+
+        dx_ref[0, :, :, :, lo:hi] = below.reshape(cap, ph, pw, hi - lo).astype(BF16)
+
+    dx_out = pltpu.make_async_copy(dx_ref, dx_hbm, out_sem.at[0])
+    dx_out.start()
 
     @pl.when(sec > 0)
     def _():
-        relay_copy().start()
-        for off in range(1, D):
-            d_copy(off).start()
+        for q in range(2):
+            start_gather(q)
 
     @pl.when(sec == last)
     def _():
@@ -254,17 +321,42 @@
         for off in range(1, S):
             head_copy(off).start()
 
-    acc_ref[...] = dot(lhs_ref[rank], dg_ref[rank], 1, 0)
-
-    def gather_step(off, carry):
-        d_copy(off).wait()
-        d = source(off)
-        acc_ref[...] += dot(lhs_ref[d], dg_ref[d], 1, 0)
+    def add_block(d, q):
+        acc[q][...] += dot(lhs_ref[d], dg[q][d], 1, 0)
+
+    for q in range(2):
+        acc[q][...] = dot(lhs_ref[rank], dg[q][rank], 1, 0)
+
+    def far_step(off, carry):
+        for q in range(2):
+            far_copy(q, off).wait()
+            forward(q, off).start()
+        for q in range(2):
+            add_block(far_source(off) + core, q)
         return carry
 
-    lax.fori_loop(1, D, gather_step, 0)
-    for t in range(9):
-        wg_ref[t] = acc_ref[t * cp : t * cp + cw, :]
+    lax.fori_loop(1, C, far_step, 0)
+
+    for q in range(2):
+        near_copy(q).wait()
+        add_block(partner, q)
+
+    def forward_step(off, carry):
+        for q in range(2):
+            forward(q, off).wait()
+            add_block(far_source(off) + 1 - core, q)
+        return carry
+
+    lax.fori_loop(1, C, forward_step, 0)
+    wg_out = []
+    for i in range(3):
+        for t in range(3 * i, 3 * i + 3):
+            for q, (lo, hi) in enumerate(span):
+                wg_ref[t, :, lo:hi] = acc[q][t * cp : t * cp + cw, :]
+        part_i = pl.ds(3 * i, 3)
+        cpy = pltpu.make_async_copy(wg_ref.at[part_i], wg_hbm.at[part_i], out_sem.at[2 + i])
+        cpy.start()
+        wg_out.append(cpy)
 
     @pl.when(sec == last)
     def _():
@@ -277,9 +369,28 @@
         head_copy(1).wait_recv()
         hg_ref[...] = hgr_ref[0:cw, :]
 
+    hg_out = pltpu.make_async_copy(hg_ref, hg_hbm, out_sem.at[1])
+    hg_out.start()
+    for cpy in [dx_out, hg_out] + wg_out:
+        cpy.wait()
+
     @pl.when(sec > 0)
     def _():
-        relay_copy().wait_send()
+        for q in range(2):
+            relay_copy(q).wait_send()
+
+
+def leave(a_ref, b_ref, c_ref, ao_ref, bo_ref, co_ref, sems):
+    copies = [
+        pltpu.make_async_copy(b_ref.at[pl.ds(i, 1)], bo_ref.at[pl.ds(i, 1)], sems.at[2 + i])
+        for i in range(9)
+    ]
+    copies.append(pltpu.make_async_copy(a_ref, ao_ref, sems.at[0]))
+    copies.append(pltpu.make_async_copy(c_ref, co_ref, sems.at[1]))
+    for cpy in copies:
+        cpy.start()
+    for cpy in copies:
+        cpy.wait()
 
 
 def per_device(mesh_sizes, saved, kernels, head, counts, pairs, valid):
@@ -288,25 +399,40 @@
     emb = head.shape[1]
     cw = ch // D
     cp = -(-cw // 16) * 16
+    c0 = (ch - 1) // 256 * 256
+    c1 = ch - c0
     rows = cap * ph * pw
     taps = jnp.transpose(kernels[0], (1, 2, 0, 3)).reshape(9, ch, ch)
-    cfg = (S, D, cap, ph, pw, ch, emb, cw, cp)
-    vmem = pl.BlockSpec(memory_space=pltpu.VMEM)
-    smem = pl.BlockSpec(memory_space=pltpu.SMEM)
+    cfg = (S, D, cap, ph, pw, ch, emb, cw, cp, c0)
+    hbm = pl.BlockSpec(memory_space=HBM)
     sem = pltpu.SemaphoreType.DMA
-    dx, wg, hg = pl.pallas_call(
+    shapes = (
+        jax.ShapeDtypeStruct((1, cap, ph, pw, ch), BF16),
+        jax.ShapeDtypeStruct((9, cw, ch), F32),
+        jax.ShapeDtypeStruct((cw, emb // S), F32),
+    )
+    results = pl.pallas_call(
         functools.partial(body, cfg),
-        out_shape=(
-            jax.ShapeDtypeStruct((1, cap, ph, pw, ch), BF16),
-            jax.ShapeDtypeStruct((9, cw, ch), F32),
-            jax.ShapeDtypeStruct((cw, emb // S), F32),
-        ),
-        in_specs=[vmem, pl.BlockSpec(memory_space=pl.ANY), vmem, smem, smem, smem],
-        out_specs=(vmem, vmem, vmem),
+        out_shape=shapes,
+        in_specs=[hbm] * 6,
+        out_specs=(hbm,) * 3,
         scratch_shapes=[
+            pltpu.VMEM(shapes[0].shape, BF16),
+            pltpu.VMEM(shapes[1].shape, F32),
+            pltpu.VMEM(shapes[2].shape, F32),
+            sem((5,)),
+            pltpu.VMEM(saved.shape, BF16),
+            pltpu.VMEM(head.shape, BF16),
+            pltpu.SMEM(counts.shape, jnp.int32),
+            pltpu.SMEM(pairs.shape, jnp.int32),
+            pltpu.SMEM(valid.shape, jnp.int32),
             pltpu.VMEM((9, ch, ch), BF16),
-            pltpu.VMEM((9 * ch, ch), BF16),
+            pltpu.VMEM((9 * c0, ch), BF16),
+            pltpu.VMEM((9 * c1, ch), BF16),
             pltpu.VMEM((rows, 9 * ch), BF16),
+            pltpu.VMEM((rows, 9 * c0), BF16),
+            pltpu.VMEM((rows, 9 * c1), BF16),
+            pltpu.VMEM((rows, ch), F32),
             pltpu.VMEM((rows, ch), F32),
             pltpu.VMEM((8, ch + 128), F32),
             pltpu.VMEM((D, 8, ch + 128), F32),
@@ -317,22 +443,36 @@
             pltpu.VMEM((D, cp, rows), BF16),
             pltpu.VMEM((D, cp, rows), BF16),
             pltpu.VMEM((D, 9 * cp, rows), BF16),
-            pltpu.VMEM((D, rows, ch), BF16),
-            pltpu.VMEM((9 * cp, ch), F32),
-            pltpu.VMEM((rows, ch), F32),
-            pltpu.VMEM((rows, ch), BF16),
-            pltpu.VMEM((rows, ch), BF16),
+            pltpu.VMEM((D, rows, c0), BF16),
+            pltpu.VMEM((D, rows, c1), BF16),
+            pltpu.VMEM((9 * cp, c0), F32),
+            pltpu.VMEM((9 * cp, c1), F32),
+            pltpu.VMEM((8, ch), F32),
+            pltpu.VMEM((rows, c0), BF16),
+            pltpu.VMEM((rows, c1), BF16),
+            pltpu.VMEM((rows, c0), BF16),
+            pltpu.VMEM((rows, c1), BF16),
+            sem((5,)),
             sem((3,)),
             sem((D - 1,)), sem((D - 1,)),
             sem((S - 1,)), sem((1,)),
             sem((D - 1,)), sem((D - 1,)),
-            sem((D - 1,)), sem((D - 1,)),
-            sem((1,)), sem((1,)),
+            sem((2, D // 2)), sem((2, D // 2)),
+            sem((2, D // 2)), sem((2, D // 2)),
+            sem((2,)), sem((2,)),
         ],
         compiler_params=pltpu.CompilerParams(
-            collective_id=0, has_side_effects=True, vmem_limit_bytes=50 * 2**20
+            collective_id=0, has_side_effects=True, vmem_limit_bytes=60 * 2**20
         ),
     )(saved, taps, head, counts, pairs, valid)
+    dx, wg, hg = pl.pallas_call(
+        leave,
+        out_shape=shapes,
+        in_specs=[hbm] * 3,
+        out_specs=(hbm,) * 3,
+        scratch_shapes=[sem((11,))],
+        compiler_params=pltpu.CompilerParams(vmem_limit_bytes=60 * 2**20),
+    )(*results)
     wgrad = jnp.transpose(wg.reshape(3, 3, cw, ch), (2, 0, 1, 3))
     return dx, wgrad[None], hg
 

time: 43.2 us -> 59.4 us (1.37)
  the two profiles are of different devices: /device:TPU:1 before, /device:TPU:0 now
where the time goes in v2:
time: 59.4 us; the launch traced here: 59.3 us
  Pallas kernels  58 us (98%)
  between operations  1.29 us (2%)
    pallas_call x1, Pallas kernels, per_device(): pl.pallas_call(functools.partial(body, cfg), out_shape=shapes, in_specs=[...  33 us
    pallas_call x1, Pallas kernels, per_device(): pl.pallas_call(leave, out_shape=shapes, in_specs=[hbm] * 3, out_specs=(hb...  25 us

profile of v2, /device:TPU:0, one launch (start us, length us, event | category | flops | bytes accessed | tf_op | source)
XLA Modules:
  0.0 59.3 jit_solution(16108386945835395864)
XLA Ops:
  1.3 33.0 %shard_map.85 = (bf16[1,4,4,8,384]{4,3,2,1,0:T(8,128)(2,1)}, f32[9,48,384]{2,1,0:T(8,128)}, f32[48,128]{1,0:T(8,128)}) custom-call(bf16[1,4,4,8,384]{4,3,2,1,0:T(8,128)(2,1)} %x_hbm.1, bf16[9,384,384]{2,1,0:T(8,128)(2,1)} %bitcast.10, bf16[384,512]{1,0:T(8,128)(2,1)} %head_hbm.1, s32[1]{0:T(128)S(6)} %copy.9.counts_hbm, s32[4]{0:T(128)} %pairs_hbm.1, s32[4]{0:T(128)} %valid_hbm.1), custom_call_target="tpu_custom_call" | custom-call | tf_op jit(solution)/shard_map/pallas_call | solution.py:414
  34.3 25.0 %shard_map.86 = (bf16[1,4,4,8,384]{4,3,2,1,0:T(8,128)(2,1)}, f32[9,48,384]{2,1,0:T(8,128)}, f32[48,128]{1,0:T(8,128)}) custom-call(bf16[1,4,4,8,384]{4,3,2,1,0:T(8,128)(2,1)} %get-tuple-element.9.a_ref, f32[9,48,384]{2,1,0:T(8,128)} %get-tuple-element.10.b_ref, f32[48,128]{1,0:T(8,128)} %get-tuple-element.11.c_ref), custom_call_target="tpu_custom_call" | custom-call | tf_op jit(solution)/shard_map/pallas_call | solution.py:468

commit v3 on v2

--- a/solution.py
+++ b/solution.py
@@ -47,7 +47,7 @@
 
 
 def body(cfg, x_hbm, k_hbm, head_hbm, counts_hbm, pairs_hbm, valid_hbm,
-         dx_hbm, wg_hbm, hg_hbm, dx_ref, wg_ref, hg_ref, out_sem,
+         dx_ref, wg_ref, hg_ref,
          x_ref, head_ref, counts_ref, pairs_ref, valid_ref,
          k_ref, kt0_ref, kt1_ref, patch_ref, patch0_ref, patch1_ref, part_ref, slope_ref,
          pooled_ref, g_ref, dproj_ref, pt_ref,
@@ -147,15 +147,20 @@
             send_sem=xs_sem.at[off - 1], recv_sem=xr_sem.at[off - 1],
             device_id=(sec, peer(off)), device_id_type=MESH)
 
-    xt = x.T
-    for p in range(D):
-        blk = xt[p * cw : (p + 1) * cw]
-        if cp != cw:
-            blk = jnp.concatenate([blk, jnp.zeros((cp - cw, rows), F32)], axis=0)
-        xt_ref[p] = blk.astype(BF16)
-    xg_ref[rank] = xt_ref[rank]
-    for off in range(1, D):
-        x_copy(off).start()
+    def send_inputs():
+        xt = x_ref[0].astype(F32).reshape(rows, ch).T
+        for p in range(D):
+            blk = xt[p * cw : (p + 1) * cw]
+            if cp != cw:
+                blk = jnp.concatenate([blk, jnp.zeros((cp - cw, rows), F32)], axis=0)
+            xt_ref[p] = blk.astype(BF16)
+        xg_ref[rank] = xt_ref[rank]
+        for off in range(1, D):
+            x_copy(off).start()
+
+    @pl.when(sec != last)
+    def _():
+        send_inputs()
 
     for t in range(9):
         kt_t = k_ref[t].T
@@ -298,13 +303,14 @@
 
         dx_ref[0, :, :, :, lo:hi] = below.reshape(cap, ph, pw, hi - lo).astype(BF16)
 
-    dx_out = pltpu.make_async_copy(dx_ref, dx_hbm, out_sem.at[0])
-    dx_out.start()
-
     @pl.when(sec > 0)
     def _():
         for q in range(2):
             start_gather(q)
+
+        @pl.when(sec == last)
+        def _():
+            send_inputs()
 
     @pl.when(sec == last)
     def _():
@@ -348,15 +354,9 @@
         return carry
 
     lax.fori_loop(1, C, forward_step, 0)
-    wg_out = []
-    for i in range(3):
-        for t in range(3 * i, 3 * i + 3):
-            for q, (lo, hi) in enumerate(span):
-                wg_ref[t, :, lo:hi] = acc[q][t * cp : t * cp + cw, :]
-        part_i = pl.ds(3 * i, 3)
-        cpy = pltpu.make_async_copy(wg_ref.at[part_i], wg_hbm.at[part_i], out_sem.at[2 + i])
-        cpy.start()
-        wg_out.append(cpy)
+    for q, (lo, hi) in enumerate(span):
+        for t in range(9):
+            wg_ref[t, :, lo:hi] = acc[q][t * cp : t * cp + cw, :]
 
     @pl.when(sec == last)
     def _():
@@ -368,11 +368,6 @@
     def _():
         head_copy(1).wait_recv()
         hg_ref[...] = hgr_ref[0:cw, :]
-
-    hg_out = pltpu.make_async_copy(hg_ref, hg_hbm, out_sem.at[1])
-    hg_out.start()
-    for cpy in [dx_out, hg_out] + wg_out:
-        cpy.wait()
 
     @pl.when(sec > 0)
     def _():
@@ -405,6 +400,7 @@
     taps = jnp.transpose(kernels[0], (1, 2, 0, 3)).reshape(9, ch, ch)
     cfg = (S, D, cap, ph, pw, ch, emb, cw, cp, c0)
     hbm = pl.BlockSpec(memory_space=HBM)
+    vmem = pl.BlockSpec(memory_space=pltpu.VMEM)
     sem = pltpu.SemaphoreType.DMA
     shapes = (
         jax.ShapeDtypeStruct((1, cap, ph, pw, ch), BF16),
@@ -413,14 +409,10 @@
     )
     results = pl.pallas_call(
         functools.partial(body, cfg),
-        out_shape=shapes,
+        out_shape=tuple(pltpu.VMEM(v.shape, v.dtype) for v in shapes),
         in_specs=[hbm] * 6,
-        out_specs=(hbm,) * 3,
+        out_specs=(vmem,) * 3,
         scratch_shapes=[
-            pltpu.VMEM(shapes[0].shape, BF16),
-            pltpu.VMEM(shapes[1].shape, F32),
-            pltpu.VMEM(shapes[2].shape, F32),
-            sem((5,)),
             pltpu.VMEM(saved.shape, BF16),
             pltpu.VMEM(head.shape, BF16),
             pltpu.SMEM(counts.shape, jnp.int32),
@@ -462,16 +454,16 @@
             sem((2,)), sem((2,)),
         ],
         compiler_params=pltpu.CompilerParams(
-            collective_id=0, has_side_effects=True, vmem_limit_bytes=60 * 2**20
+            collective_id=0, has_side_effects=True, vmem_limit_bytes=58 * 2**20
         ),
     )(saved, taps, head, counts, pairs, valid)
     dx, wg, hg = pl.pallas_call(
         leave,
         out_shape=shapes,
-        in_specs=[hbm] * 3,
+        in_specs=[vmem] * 3,
         out_specs=(hbm,) * 3,
         scratch_shapes=[sem((11,))],
-        compiler_params=pltpu.CompilerParams(vmem_limit_bytes=60 * 2**20),
+        compiler_params=pltpu.CompilerParams(vmem_limit_bytes=4 * 2**20),
     )(*results)
     wgrad = jnp.transpose(wg.reshape(3, 3, cw, ch), (2, 0, 1, 3))
     return dx, wgrad[None], hg

time: 59.4 us -> 33.8 us (0.57)
  Pallas kernels: 58 us -> 32.4 us
    pallas_call x2, Pallas kernels: 58 us -> 32.4 us  [the longest x1 31.4 us: per_device(): pl.pallas_call(functools.partial(body, cfg), out_shape=tuple((pltpu.VMEM(...]
where the time goes in v3:
time: 33.8 us; the launch traced here: 33.7 us
  Pallas kernels  32.4 us (96%)
  between operations  1.29 us (4%)
    pallas_call x1, Pallas kernels, per_device(): pl.pallas_call(functools.partial(body, cfg), out_shape=tuple((pltpu.VMEM(...  31.4 us
    pallas_call x1, Pallas kernels, per_device(): pl.pallas_call(leave, out_shape=shapes, in_specs=[vmem] * 3, out_specs=(h...  0.96 us

profile of v3, /device:TPU:0, one launch (start us, length us, event | category | flops | bytes accessed | tf_op | source)
XLA Modules:
  0.0 33.7 jit_solution(12332062895397919275)
XLA Ops:
  1.3 31.4 %shard_map.85 = (bf16[1,4,4,8,384]{4,3,2,1,0:T(8,128)(2,1)S(1)}, f32[9,48,384]{2,1,0:T(8,128)S(1)}, f32[48,128]{1,0:T(8,128)S(1)}) custom-call(bf16[1,4,4,8,384]{4,3,2,1,0:T(8,128)(2,1)} %x_hbm.1, bf16[9,384,384]{2,1,0:T(8,128)(2,1)} %bitcast.10, bf16[384,512]{1,0:T(8,128)(2,1)} %head_hbm.1, s32[1]{0:T(128)S(6)} %copy.9.counts_hbm, s32[4]{0:T(128)} %pairs_hbm.1, ...), custom_call_target="tpu_custom_call" | custom-call | tf_op jit(solution)/shard_map/pallas_call | solution.py:410
  32.7 1.0 %shard_map.86 = (bf16[1,4,4,8,384]{4,3,2,1,0:T(8,128)(2,1)}, f32[9,48,384]{2,1,0:T(8,128)}, f32[48,128]{1,0:T(8,128)}) custom-call(bf16[1,4,4,8,384]{4,3,2,1,0:T(8,128)(2,1)S(1)} %get-tuple-element.9.a_ref, f32[9,48,384]{2,1,0:T(8,128)S(1)} %get-tuple-element.10.b_ref, f32[48,128]{1,0:T(8,128)S(1)} %get-tuple-element.11.c_ref), custom_call_target="tpu_custom_call" | custom-call | tf_op jit(solution)/shard_map/pallas_call | solution.py:460

commit v4 on v3

--- a/solution.py
+++ b/solution.py
@@ -333,22 +333,28 @@
     for q in range(2):
         acc[q][...] = dot(lhs_ref[rank], dg[q][rank], 1, 0)
 
+    for q in range(2):
+        near_copy(q).wait()
+        add_block(partner, q)
+
     def far_step(off, carry):
         for q in range(2):
-            far_copy(q, off).wait()
+            far_copy(q, off).wait_recv()
             forward(q, off).start()
+        return carry
+
+    lax.fori_loop(1, C, far_step, 0)
+
+    def far_add(off, carry):
         for q in range(2):
             add_block(far_source(off) + core, q)
         return carry
 
-    lax.fori_loop(1, C, far_step, 0)
-
-    for q in range(2):
-        near_copy(q).wait()
-        add_block(partner, q)
+    lax.fori_loop(1, C, far_add, 0)
 
     def forward_step(off, carry):
         for q in range(2):
+            far_copy(q, off).wait_send()
             forward(q, off).wait()
             add_block(far_source(off) + 1 - core, q)
         return carry

time: 33.8 us -> 33.6 us (level)
  no operation moved by 1% of the time
where the time goes in v4:
time: 33.6 us; the launch traced here: 33.4 us
  Pallas kernels  32.1 us (96%)
  between operations  1.29 us (4%)
    pallas_call x1, Pallas kernels, per_device(): pl.pallas_call(functools.partial(body, cfg), out_shape=tuple((pltpu.VMEM(...  31.2 us
    pallas_call x1, Pallas kernels, per_device(): pl.pallas_call(leave, out_shape=shapes, in_specs=[vmem] * 3, out_specs=(h...  0.96 us

profile of v4, /device:TPU:0, one launch (start us, length us, event | category | flops | bytes accessed | tf_op | source)
XLA Modules:
  0.0 33.4 jit_solution(13975557553448944875)
XLA Ops:
  1.3 31.2 %shard_map.85 = (bf16[1,4,4,8,384]{4,3,2,1,0:T(8,128)(2,1)S(1)}, f32[9,48,384]{2,1,0:T(8,128)S(1)}, f32[48,128]{1,0:T(8,128)S(1)}) custom-call(bf16[1,4,4,8,384]{4,3,2,1,0:T(8,128)(2,1)} %x_hbm.1, bf16[9,384,384]{2,1,0:T(8,128)(2,1)} %bitcast.10, bf16[384,512]{1,0:T(8,128)(2,1)} %head_hbm.1, s32[1]{0:T(128)S(6)} %copy.9.counts_hbm, s32[4]{0:T(128)} %pairs_hbm.1, ...), custom_call_target="tpu_custom_call" | custom-call | tf_op jit(solution)/shard_map/pallas_call | solution.py:416
  32.4 1.0 %shard_map.86 = (bf16[1,4,4,8,384]{4,3,2,1,0:T(8,128)(2,1)}, f32[9,48,384]{2,1,0:T(8,128)}, f32[48,128]{1,0:T(8,128)}) custom-call(bf16[1,4,4,8,384]{4,3,2,1,0:T(8,128)(2,1)S(1)} %get-tuple-element.9.a_ref, f32[9,48,384]{2,1,0:T(8,128)S(1)} %get-tuple-element.10.b_ref, f32[48,128]{1,0:T(8,128)S(1)} %get-tuple-element.11.c_ref), custom_call_target="tpu_custom_call" | custom-call | tf_op jit(solution)/shard_map/pallas_call | solution.py:466
